TPU v7x, 256 devices: a whole 4x4x8 slice. The times are simulated.
256 devices in a mesh: energy: 64 (over z_lo, y, x), mom: 2 (over core), tile: 2 (over z_hi).
Axes of the slice: x: 4, y: 4, z: 8 (z_hi: 2, z_lo: 4; z = z_hi * 4 + z_lo), core: 2. Of those that a mesh axis runs over, the one named last changes fastest.
Arguments:
- green: float32 [2, 128, 256, 512], P('mom', ('energy', 'tile')), may hold values from -1.5 to 1.5
- phonon: float32 [256, 256], P(('energy', 'tile')), may hold values from -0.18 to 0.18
- lag_offsets: int32 [32], replicated, may hold values from -32 to 32
- grad_table: float32 [64, 256], replicated, may hold values from -1.5 to 1.5
- neighbor_grad: int32 [256, 4], P(('energy', 'tile')), may hold values from 0 to 63
Outputs:
- sigma: float32 [2, 128, 256, 512], P('mom', ('energy', 'tile'))
- green_next: float32 [2, 128, 256, 512], P('mom', ('energy', 'tile'))
All inputs are finite; a program needn't handle non-finite values.
Results may differ from a plain program's by a relative error of at most 0.000078.
Values sent between devices are 32-bit elements; how exact they have to be, the bound alone decides.
A program may use at most 64 MiB of HBM per device.

v0:
```python
import functools

import jax
import jax.numpy as jnp
from jax import lax
from jax.experimental import pallas as pl
from jax.experimental.pallas import tpu as pltpu
from jax.sharding import PartitionSpec as P

MESH = pl.DeviceIdType.MESH
EXACT = lax.Precision.HIGHEST
F32, BF16 = jnp.float32, jnp.bfloat16
NE = 128
PAIRS = 128
NBR = 4


def split(value):
    high = value.astype(BF16)
    return high, (value - high.astype(F32)).astype(BF16)


def iota(shape, dim):
    return lax.broadcasted_iota(jnp.int32, shape, dim)


def coordinates():
    energy = lax.axis_index("energy")
    return (
        energy // 16 + 4 * lax.axis_index("tile"),
        (energy // 4) % 4,
        energy % 4,
        lax.axis_index("mom"),
    )


def device_at(z, y, x):
    return {"energy": (z % 4) * 16 + y * 4 + x, "tile": z // 4}


def flat_at(z, y, x):
    return ((z % 4) * 16 + y * 4 + x) * 2 + z // 4


def lines(z, y, x):
    along_z = [device_at((z + step) % 8, y, x) for step in range(1, 8)]
    along_y = [device_at(z, (y + step) % 4, x) for step in range(1, 4)]
    along_x = [device_at(z, y, (x + step) % 4) for step in range(1, 4)]
    return along_z, along_y, along_x


def signal(sem, device):
    pl.semaphore_signal(sem, inc=1, device_id=device, device_id_type=MESH)


def tile_rows(block):
    return pl.ds(pl.multiple_of(block * 8, 8), 8)


def exchange_start(position, source, landing, send_sem, recv_sem, shift_target):
    z, y, x = position
    here = tile_rows(flat_at(z, y, x))
    depth = [((z + step) % 8) for step in range(8)]

    def send(zz, yy, xx):
        pltpu.make_async_remote_copy(
            src_ref=source.at[tile_rows(flat_at(zz, yy, xx))],
            dst_ref=landing.at[here],
            send_sem=send_sem,
            recv_sem=recv_sem,
            device_id=device_at(zz, yy, xx),
            device_id_type=MESH,
        ).start()

    for zz in depth[1:]:
        send(zz, y, x)

    @pl.loop(1, 16)
    def _(k):
        yy = (y + k // 4) % 4
        xx = (x + k % 4) % 4
        for zz in depth:
            send(zz, yy, xx)

    landing[here, :] = source[here, :]


def exchange_descriptor(source, landing, send_sem, recv_sem, device):
    rows = pl.ds(0, 8 * 127)
    return pltpu.make_async_remote_copy(
        src_ref=source.at[rows],
        dst_ref=landing.at[rows],
        send_sem=send_sem,
        recv_sem=recv_sem,
        device_id=device,
        device_id_type=MESH,
    )


def build_weights(core, phonon, lags, whi, wlo):
    place = (iota((256, 32), 0) // 4) % 32 == iota((256, 32), 1)
    lag_column = jnp.sum(
        jnp.where(place, jnp.broadcast_to(lags[...], (256, 32)), 0), axis=1, keepdims=True
    )
    lane = iota((256, 256), 1)
    offset = jnp.where(lane < 128, lane, lane - 256)
    picked = jnp.where(offset == -lag_column, 1.0, 0.0).astype(F32)
    row, column = iota((8, 256), 0), iota((8, 256), 1)
    mine = (column // 128 == row // 4) & (column % 4 == row % 4)
    coeffs = jnp.where(mine, jnp.broadcast_to(phonon[pl.ds(core, 1), :], (8, 256)), 0.0)
    profile = jnp.dot(coeffs, picked, precision=EXACT, preferred_element_type=F32)
    for q in range(2):
        for n in range(NBR):
            spread = jnp.broadcast_to(profile[q * 4 + n : q * 4 + n + 1, :], (128, 256))
            toeplitz = pltpu.roll(spread, 0, 1, stride=1, stride_axis=0)[:, :128]
            high, low = split(toeplitz)
            for k in range(2):
                rows = slice(n * 256 + k * 128, n * 256 + k * 128 + 128)
                cols = slice(((k + q) % 2) * 128, ((k + q) % 2) * 128 + 128)
                whi[rows, cols] = high
                wlo[rows, cols] = low


def build_kron(core, neighbor, grad, khi, klo, factors):
    column = iota((16, 256), 1)
    mine = column % 16 == iota((16, 256), 0)
    source, target = iota((256, 256), 0), iota((256, 256), 1)
    outer = jnp.where(source // 16 == target // 16, 1.0, 0.0).astype(F32)
    inner = jnp.where(source // 16 == target % 16, 1.0, 0.0).astype(F32)
    for n in range(NBR):
        block = jnp.broadcast_to(grad[pl.ds(neighbor[core, n], 1), :], (16, 256))
        factors[n * 16 : n * 16 + 16, :] = jnp.where(mine, block, 0.0)
    left = factors[...]
    first = jnp.dot(left, outer, precision=EXACT, preferred_element_type=F32)
    second = jnp.dot(left, inner, precision=EXACT, preferred_element_type=F32)
    for n in range(NBR):
        for j in range(16):
            row = first[n * 16 + j : n * 16 + j + 1, :]
            high, low = split(row * second[n * 16 : n * 16 + 16, :])
            rows = slice(n * 256 + j * 16, n * 256 + j * 16 + 16)
            khi[rows, :] = high
            klo[rows, :] = low


def contract(got, xhi, xlo, whi, wlo, khi, klo, hhi, hlo, result):
    for k in range(2):
        for t in range(4):
            high, low = split(got[pl.ds(k * 4 + t, NE, stride=8), :])
            rows, cols = slice(k * 128, k * 128 + 128), slice(t * 128, t * 128 + 128)
            xhi[rows, cols] = high
            xlo[rows, cols] = low
    high, low = xhi[...], xlo[...]
    right = jnp.concatenate([high, low, high], axis=0)

    @pl.loop(0, NBR)
    def _(n):
        rows = pl.ds(pl.multiple_of(n * 256, 256), 256)
        wh, wl = whi[rows, :], wlo[rows, :]
        mixed = jnp.dot(
            jnp.concatenate([wh, wh, wl], axis=1), right, preferred_element_type=F32
        )
        high, low = split(mixed)
        hhi[n] = high
        hlo[n] = low

    for part in range(2):
        cols = slice(part * 256, part * 256 + 256)
        total = None
        for n in range(NBR):
            rows = slice(n * 256, n * 256 + 256)
            kh, kl = khi[rows, :], klo[rows, :]
            hh, hl = hhi[n, :, cols], hlo[n, :, cols]
            term = jnp.dot(
                jnp.concatenate([hh, hh, hl], axis=1),
                jnp.concatenate([kh, kl, kh], axis=0),
                preferred_element_type=F32,
            )
            total = term if total is None else total + term
        for k in range(2):
            for half in range(2):
                result[pl.ds(k * 4 + part * 2 + half, NE, stride=8), :] = total[
                    k * 128 : k * 128 + 128, half * 128 : half * 128 + 128
                ]


def load_columns(source, target, sems):
    loads = [
        pltpu.make_async_copy(
            source.at[:, pl.ds(t * 128, 128)], target.at[pl.ds(t * 256, 256)], sems.at[t]
        )
        for t in range(4)
    ]
    for load in loads:
        load.start()
    return loads


def scatter_kernel(
    green, phonon, lags, grad, neighbor, sigma,
    held, swap_out, swap_in, stage, got, result, back, whi, wlo, khi, klo, factors, xhi, xlo, hhi, hlo,
    send_sems, recv_sems, stage_sems, load_sem,
):
    loads = load_columns(green, held, load_sem)
    z, y, x, core = coordinates()
    position = (z, y, x)
    sibling = {"mom": 1 - core}
    along_z, along_y, along_x = lines(z, y, x)
    barrier = pltpu.get_barrier_semaphore()
    for device in [sibling] + along_z + along_y + along_x:
        signal(barrier, device)

    for load in loads:
        load.wait()
    for t in range(4):
        swap_out[t] = held[pl.ds(t * 256 + 1 - core, PAIRS, stride=2), :]
        stage[pl.ds(core * 4 + t, PAIRS, stride=8), :] = held[
            pl.ds(t * 256 + core, PAIRS, stride=2), :
        ]
    pl.semaphore_wait(barrier, 14)

    swap = pltpu.make_async_remote_copy(
        src_ref=swap_out, dst_ref=swap_in, send_sem=send_sems.at[0], recv_sem=recv_sems.at[0],
        device_id=sibling, device_id_type=MESH,
    )
    swap.start()
    for device in along_y:
        signal(stage_sems.at[0], device)
    build_weights(core, phonon, lags, whi, wlo)
    pl.semaphore_wait(stage_sems.at[0], 3)
    for device in along_x:
        signal(stage_sems.at[1], device)
    swap.wait()
    for t in range(4):
        stage[pl.ds((1 - core) * 4 + t, PAIRS, stride=8), :] = swap_in[t]
    pl.semaphore_wait(stage_sems.at[1], 3)

    exchange_start(position, stage, got, send_sems.at[1], recv_sems.at[1], None)
    build_kron(core, neighbor, grad, khi, klo, factors)
    exchange_descriptor(stage, got, send_sems.at[1], recv_sems.at[1], sibling).wait()
    contract(got, xhi, xlo, whi, wlo, khi, klo, hhi, hlo, result)
    exchange_start(position, result, back, send_sems.at[2], recv_sems.at[2], None)
    exchange_descriptor(result, back, send_sems.at[2], recv_sems.at[2], sibling).wait()

    for t in range(4):
        swap_out[t] = back[pl.ds((1 - core) * 4 + t, PAIRS, stride=8), :]
    swap_back = pltpu.make_async_remote_copy(
        src_ref=swap_out, dst_ref=sigma.at[1], send_sem=send_sems.at[3], recv_sem=recv_sems.at[3],
        device_id=sibling, device_id_type=MESH,
    )
    swap_back.start()
    for t in range(4):
        sigma[0, t] = back[pl.ds(core * 4 + t, PAIRS, stride=8), :]
    swap_back.wait()


def scatter(green, phonon, lags, grad, neighbor):
    vmem = pl.BlockSpec(memory_space=pltpu.VMEM)
    return pl.pallas_call(
        scatter_kernel,
        out_shape=jax.ShapeDtypeStruct((2, 4, PAIRS, 128), F32),
        in_specs=[pl.BlockSpec(memory_space=pl.ANY)] + [vmem] * 3 + [pl.BlockSpec(memory_space=pltpu.SMEM)],
        out_specs=vmem,
        scratch_shapes=[
            pltpu.VMEM((1024, 128), F32),
            pltpu.VMEM((4, PAIRS, 128), F32),
            pltpu.VMEM((4, PAIRS, 128), F32),
            pltpu.VMEM((1024, 128), F32),
            pltpu.VMEM((1024, 128), F32),
            pltpu.VMEM((1024, 128), F32),
            pltpu.VMEM((1024, 128), F32),
            pltpu.VMEM((1024, 256), BF16),
            pltpu.VMEM((1024, 256), BF16),
            pltpu.VMEM((1024, 256), BF16),
            pltpu.VMEM((1024, 256), BF16),
            pltpu.VMEM((64, 256), F32),
            pltpu.VMEM((256, 512), BF16),
            pltpu.VMEM((256, 512), BF16),
            pltpu.VMEM((NBR, 256, 512), BF16),
            pltpu.VMEM((NBR, 256, 512), BF16),
            pltpu.SemaphoreType.DMA((4,)),
            pltpu.SemaphoreType.DMA((4,)),
            pltpu.SemaphoreType.REGULAR((2,)),
            pltpu.SemaphoreType.DMA((4,)),
        ],
        compiler_params=pltpu.CompilerParams(
            collective_id=0, has_side_effects=True, vmem_limit_bytes=40 * 1024 * 1024
        ),
        cost_estimate=pl.CostEstimate(
            flops=2 * 10**9, bytes_accessed=4 * 10**6, transcendentals=0
        ),
    )(green, phonon, lags, grad, neighbor)


def complex_rows(target, left, right, base):
    @pl.loop(0, 4)
    def _(block):
        first = pl.multiple_of(block * 64, 64)
        real = [None] * 4
        imag = [None] * 4
        for j in range(16):
            b_real = right[j * 16 : j * 16 + 16, :]
            b_imag = right[256 + j * 16 : 256 + j * 16 + 16, :]
            for i in range(4):
                a_real = left[pl.ds(first + i * 16 + j, 1), :]
                a_imag = left[pl.ds(256 + first + i * 16 + j, 1), :]
                add_real = a_real * b_real - a_imag * b_imag
                add_imag = a_real * b_imag + a_imag * b_real
                real[i] = add_real if j == 0 else real[i] + add_real
                imag[i] = add_imag if j == 0 else imag[i] + add_imag
        for i in range(4):
            rows = pl.ds(first + i * 16, 16)
            late = pl.ds(256 + first + i * 16, 16)
            if base is None:
                target[rows, :] = real[i]
                target[late, :] = imag[i]
            else:
                target[rows, :] = base[rows, :] + real[i]
                target[late, :] = base[late, :] + imag[i]


def store_columns(source, target, sems):
    stores = [
        pltpu.make_async_copy(
            source.at[pl.ds(t * 256, 256)], target.at[:, pl.ds(t * 128, 128)], sems.at[t]
        )
        for t in range(4)
    ]
    for store in stores:
        store.start()
    return stores


def dyson_kernel(
    green, blocks, sigma, after, held, summed, final, g_rows, s_rows, r_rows, x_rows,
    load_sem, sigma_sem, after_sem,
):
    core = lax.axis_index("mom")
    loads = load_columns(green, held, load_sem)
    for which in range(2):
        parity = core if which == 0 else 1 - core
        for t in range(4):
            summed[pl.ds(t * 256 + parity, PAIRS, stride=2), :] = blocks[which, t]
    stores = store_columns(summed, sigma, sigma_sem)
    for load in loads:
        load.wait()

    @pl.loop(0, 2)
    def _(parity):
        for t in range(4):
            rows = slice(t * 128, t * 128 + 128)
            atoms = pl.ds(t * 256 + parity, PAIRS, stride=2)
            s_rows[rows, :] = summed[atoms, :].T
            g_rows[rows, :] = held[atoms, :].T
        complex_rows(r_rows, g_rows, s_rows, None)
        complex_rows(x_rows, r_rows, g_rows, g_rows)
        complex_rows(s_rows, r_rows, x_rows, g_rows)
        for t in range(4):
            rows = slice(t * 128, t * 128 + 128)
            final[pl.ds(t * 256 + parity, PAIRS, stride=2), :] = s_rows[rows, :].T

    stores += store_columns(final, after, after_sem)
    for store in stores:
        store.wait()


def dyson(green, blocks):
    whole = pl.BlockSpec(memory_space=pl.ANY)
    return pl.pallas_call(
        dyson_kernel,
        out_shape=[jax.ShapeDtypeStruct((256, 512), F32)] * 2,
        in_specs=[whole, pl.BlockSpec(memory_space=pltpu.VMEM)],
        out_specs=[whole] * 2,
        scratch_shapes=[pltpu.VMEM((1024, 128), F32)] * 3
        + [pltpu.VMEM((512, 128), F32)] * 4
        + [pltpu.SemaphoreType.DMA((4,))] * 3,
        compiler_params=pltpu.CompilerParams(vmem_limit_bytes=16 * 1024 * 1024),
        cost_estimate=pl.CostEstimate(
            flops=3 * 10**7, bytes_accessed=2 * 10**6, transcendentals=0
        ),
    )(green, blocks)


def body(green, phonon, lag_offsets, grad_table, neighbor_grad):
    own = green.reshape(256, 512)
    blocks = scatter(own, phonon, lag_offsets.reshape(1, 32), grad_table, neighbor_grad)
    sigma, after = dyson(own, blocks)
    return sigma.reshape(green.shape), after.reshape(green.shape)


def solution(mesh):
    whole = P("mom", ("energy", "tile"), None, None)
    rows = P(("energy", "tile"), None)
    return jax.shard_map(
        body,
        mesh=mesh,
        in_specs=(whole, rows, P(), P(), rows),
        out_specs=(whole, whole),
        check_vma=False,
    )
```

profile of v0, /device:TPU:1, one launch (start us, length us, event | category | flops | bytes accessed | tf_op | source)
XLA Modules:
  0.0 55.8 jit_solution(14934390326139686298)
XLA Ops:
  0.6 0.0 copy-start.2
  0.6 0.0 copy-start.3
  0.7 0.0 copy-start.4
  0.7 0.7 %copy-done.2 = f32[2,256]{1,0:T(2,128)S(1)} copy-done((f32[2,256]{1,0:T(2,128)S(1)}, f32[2,256]{1,0:T(2,128)}, u32[]{:S(2)}) %copy-start.2) | copy-done | bytes 2072
  1.3 0.0 copy-done.3
  1.3 0.0 copy-done.4
  1.3 0.0 copy-start
  1.3 1.0 %copy-done = f32[1,1,256,512]{3,2,1,0:T(8,128)S(1)} copy-done((f32[1,1,256,512]{3,2,1,0:T(8,128)S(1)}, f32[1,1,256,512]{3,2,1,0:T(8,128)}, u32[]{:S(2)}) %copy-start) | copy-done | bytes 524312
  2.4 0.0 copy-start.1
  2.4 0.8 %copy-done.1 = f32[64,256]{1,0:T(8,128)S(1)} copy-done((f32[64,256]{1,0:T(8,128)S(1)}, f32[64,256]{1,0:T(8,128)}, u32[]{:S(2)}) %copy-start.1) | copy-done | bytes 65560
  3.2 47.3 %shard_map.68.blocks = f32[2,4,128,128]{3,2,1,0:T(8,128)S(1)} custom-call(f32[256,512]{1,0:T(8,128)S(1)} %bitcast.4, f32[2,256]{1,0:T(2,128)S(1)} %copy-done.2, s32[1,32]{1,0:T(1,128)S(1)} %bitcast.6, f32[64,256]{1,0:T(8,128)S(1)} %copy-done.1, s32[2,4]{1,0:T(2,128)S(1)} %copy-done.3), custom_call_target="tpu_custom_call" | custom-call | flops 2000000000 | bytes 4000000 | tf_op jit(solution)/shard_map/pallas_call | solution.py:258
  50.5 5.3 %shard_map.69 = (f32[256,512]{1,0:T(8,128)}, f32[256,512]{1,0:T(8,128)}) custom-call(f32[256,512]{1,0:T(8,128)S(1)} %bitcast.5, f32[2,4,128,128]{3,2,1,0:T(8,128)S(1)} %shard_map.68.blocks), custom_call_target="tpu_custom_call" | custom-call | flops 30000000 | bytes 2000000 | tf_op jit(solution)/shard_map/pallas_call | solution.py:368
Async XLA Ops:
  0.6 0.7 %copy-start.2 = (f32[2,256]{1,0:T(2,128)S(1)}, f32[2,256]{1,0:T(2,128)}, u32[]{:S(2)}) copy-start(f32[2,256]{1,0:T(2,128)} %phonon.1) | copy-start | bytes 6148
  0.6 0.7 %copy-start.3 = (s32[2,4]{1,0:T(2,128)S(1)}, s32[2,4]{1,0:T(2,128)}, u32[]{:S(2)}) copy-start(s32[2,4]{1,0:T(2,128)} %neighbor.1) | copy-start | bytes 100
  0.7 0.7 %copy-start.4 = (s32[32]{0:T(128)S(1)}, s32[32]{0:T(128)}, u32[]{:S(2)}) copy-start(s32[32]{0:T(128)} %param.7) | copy-start | bytes 388
  1.3 1.0 %copy-start = (f32[1,1,256,512]{3,2,1,0:T(8,128)S(1)}, f32[1,1,256,512]{3,2,1,0:T(8,128)}, u32[]{:S(2)}) copy-start(f32[1,1,256,512]{3,2,1,0:T(8,128)} %param.5) | copy-start | bytes 1572868
  2.4 0.8 %copy-start.1 = (f32[64,256]{1,0:T(8,128)S(1)}, f32[64,256]{1,0:T(8,128)}, u32[]{:S(2)}) copy-start(f32[64,256]{1,0:T(8,128)} %grad.1) | copy-start | bytes 196612
where the time goes:
time: 56.1 us; the launch traced here: 55.8 us
  Pallas kernels  52.6 us (94%)
  local copies, waits for them, and re-layouts  2.55 us (5%)
  between operations  0.67 us (1%)
    pallas_call x1, Pallas kernels, scatter(): pl.pallas_call(scatter_kernel, out_shape=jax.ShapeDtypeStruct((2, 4, PAIR...  47.3 us
    pallas_call x1, Pallas kernels, dyson(): pl.pallas_call(dyson_kernel, out_shape=[jax.ShapeDtypeStruct((256, 512),...  5.29 us
    unnamed x10, local copies, waits for them, and re-layouts  2.55 us

commit v1 on v0

v1 whole, which is shorter than its diff:
```python
import functools

import jax
import jax.numpy as jnp
from jax import lax
from jax.experimental import pallas as pl
from jax.experimental.pallas import tpu as pltpu
from jax.sharding import PartitionSpec as P

MESH = pl.DeviceIdType.MESH
EXACT = lax.Precision.HIGHEST
F32, BF16 = jnp.float32, jnp.bfloat16
NE = 128
PAIRS = 128
NBR = 4


def split(value):
    high = value.astype(BF16)
    return high, (value - high.astype(F32)).astype(BF16)


def iota(shape, dim):
    return lax.broadcasted_iota(jnp.int32, shape, dim)


def coordinates():
    energy = lax.axis_index("energy")
    return (
        energy // 16 + 4 * lax.axis_index("tile"),
        (energy // 4) % 4,
        energy % 4,
        lax.axis_index("mom"),
    )


def device_at(z, y, x):
    return {"energy": (z % 4) * 16 + y * 4 + x, "tile": z // 4}


def flat_at(z, y, x):
    return ((z % 4) * 16 + y * 4 + x) * 2 + z // 4


def neighbours(z, y, x):
    column = [device_at((z + step) % 8, y, x) for step in range(1, 8)]
    plane = [device_at(z, (y + step // 4) % 4, (x + step % 4) % 4) for step in range(1, 16)]
    return column, plane


def signal(sem, device):
    pl.semaphore_signal(sem, inc=1, device_id=device, device_id_type=MESH)


def tile_rows(block):
    return pl.ds(pl.multiple_of(block * 8, 8), 8)


def exchange_start(position, half, source, landing, send_sem, recv_sem):
    z, y, x = position
    here = tile_rows(flat_at(z, y, x))
    depth = [(z + step) % 8 for step in (0, 4, 3, 5, 2, 6, 1, 7)]

    def send(zz, yy, xx):
        pltpu.make_async_remote_copy(
            src_ref=source.at[tile_rows(flat_at(zz, yy, xx))],
            dst_ref=landing.at[here],
            send_sem=send_sem,
            recv_sem=recv_sem,
            device_id=device_at(zz, yy, xx),
            device_id_type=MESH,
        ).start()

    if half == 0:
        for zz in depth[1:]:
            send(zz, y, x)

    @pl.loop(1 - half, 8)
    def _(k):
        yy = (y + k // 2) % 4
        xx = (x + half + 2 * (k % 2)) % 4
        for zz in depth:
            send(zz, yy, xx)

    if half == 0:
        landing[here, :] = source[here, :]


def exchange_descriptor(half, source, landing, send_sem, recv_sem, device):
    rows = pl.ds(0, 8 * (63 + half))
    return pltpu.make_async_remote_copy(
        src_ref=source.at[rows],
        dst_ref=landing.at[rows],
        send_sem=send_sem,
        recv_sem=recv_sem,
        device_id=device,
        device_id_type=MESH,
    )


def build_weights(core, phonon, lags, whi, wlo):
    place = (iota((256, 32), 0) // 4) % 32 == iota((256, 32), 1)
    lag_column = jnp.sum(
        jnp.where(place, jnp.broadcast_to(lags[...], (256, 32)), 0), axis=1, keepdims=True
    )
    lane = iota((256, 256), 1)
    offset = jnp.where(lane < 128, lane, lane - 256)
    picked = jnp.where(offset == -lag_column, 1.0, 0.0).astype(F32)
    row, column = iota((8, 256), 0), iota((8, 256), 1)
    mine = (column // 128 == row // 4) & (column % 4 == row % 4)
    coeffs = jnp.where(mine, jnp.broadcast_to(phonon[pl.ds(core, 1), :], (8, 256)), 0.0)
    profile = jnp.dot(coeffs, picked, precision=EXACT, preferred_element_type=F32)
    source, target = iota((256, 256), 0), iota((256, 256), 1)
    energy = 4 * (target % 32) + 2 * (target // 128) + (target // 32) % 2
    orders = [
        jnp.where(
            (source % 128 == energy) & (source // 128 == (target // 64 + k) % 2), 1.0, 0.0
        ).astype(BF16)
        for k in range(2)
    ]
    for n in range(NBR):
        parts = [
            jnp.concatenate(
                [
                    pltpu.roll(
                        jnp.broadcast_to(profile[q * 4 + n : q * 4 + n + 1, :], (32, 256)),
                        step,
                        1,
                        stride=4,
                        stride_axis=0,
                    )[:, :128]
                    for q in range(2)
                ],
                axis=1,
            )
            for step in range(4)
        ]
        pieces = split(jnp.concatenate(parts, axis=0))
        for piece, kept in zip(pieces, (whi, wlo)):
            for k in range(2):
                moved = jnp.dot(piece, orders[k], preferred_element_type=F32).astype(BF16)
                for s in range(2):
                    rows = slice(s * 128 + k * 64, s * 128 + k * 64 + 64)
                    for other in range(2):
                        kept[other, rows, n * 128 : n * 128 + 128] = moved[
                            s * 64 : s * 64 + 64, other * 128 : other * 128 + 128
                        ]


def build_kron(core, neighbor, grad, khi, klo, factors):
    column = iota((16, 256), 1)
    mine = column % 16 == iota((16, 256), 0)
    source, target = iota((256, 256), 0), iota((256, 256), 1)
    outer = jnp.where(source // 16 == target // 16, 1.0, 0.0).astype(F32)
    inner = jnp.where(source // 16 == target % 16, 1.0, 0.0).astype(F32)
    for n in range(NBR):
        block = jnp.broadcast_to(grad[pl.ds(neighbor[core, n], 1), :], (16, 256))
        factors[n * 16 : n * 16 + 16, :] = jnp.where(mine, block, 0.0)
    left = factors[...]
    first = jnp.dot(left, outer, precision=EXACT, preferred_element_type=F32)
    second = jnp.dot(left, inner, precision=EXACT, preferred_element_type=F32)
    for n in range(NBR):
        for j in range(16):
            row = first[n * 16 + j : n * 16 + j + 1, :]
            high, low = split(row * second[n * 16 : n * 16 + 16, :])
            rows = slice(n * 256 + j * 16, n * 256 + j * 16 + 16)
            khi[rows, :] = high
            klo[rows, :] = low


def three_passes(left, right):
    lh, ll = left
    rh, rl = right
    return jnp.dot(
        jnp.concatenate([lh, lh, ll], axis=1),
        jnp.concatenate([rh, rl, rh], axis=0),
        preferred_element_type=F32,
    )


def energy_rows(s, zh, k, t):
    return pl.ds(16 * s + 8 * zh + 4 * k + t, 32, stride=32)


def sandwich_half(s, got, khi, klo, fhi, flo):
    loaded = [
        jnp.concatenate(
            [
                jnp.concatenate(
                    [got[energy_rows(s, zh, k, 2 * part + side), :] for side in range(2)], axis=1
                )
                for k in range(2)
                for zh in range(2)
            ],
            axis=0,
        )
        for part in range(2)
    ]
    left = split(jnp.concatenate(loaded, axis=0))
    for n in range(NBR):
        rows = slice(n * 256, n * 256 + 256)
        high, low = split(three_passes(left, (khi[rows, :], klo[rows, :])))
        for part in range(2):
            to, cols = slice(n * 128, n * 128 + 128), slice(part * 256, part * 256 + 256)
            fhi[to, cols] = high[part * 128 : part * 128 + 128, :]
            flo[to, cols] = low[part * 128 : part * 128 + 128, :]


def mix_half(rows, s, whi, wlo, fhi, flo):
    return three_passes((whi[s, rows, :], wlo[s, rows, :]), (fhi[...], flo[...]))


def load_columns(source, target, sems):
    loads = [
        pltpu.make_async_copy(
            source.at[:, pl.ds(t * 128, 128)], target.at[pl.ds(t * 256, 256)], sems.at[t]
        )
        for t in range(4)
    ]
    for load in loads:
        load.start()
    return loads


def atom_rows(t, s, zh, parity):
    return pl.ds(t * 256 + 4 * s + 2 * zh + parity, 32, stride=8)


def block_rows(t, zh, parity):
    return pl.ds(pl.multiple_of(t * 128 + zh * 64 + parity * 32, 32), 32)


QUARTERS = [(t, zh, parity) for t in range(4) for zh in range(2) for parity in range(2)]


def pick_half(source, target, s):
    for t, zh, parity in QUARTERS:
        target[block_rows(t, zh, parity), :] = source[atom_rows(t, s, zh, parity), :]


def place_half(source, target, s):
    for t, zh, parity in QUARTERS:
        target[atom_rows(t, s, zh, parity), :] = source[block_rows(t, zh, parity), :]


def turn(source, target):
    for t in range(4):
        rows = slice(t * 128, t * 128 + 128)
        target[rows, :] = source[rows, :].T


def dyson_rows(g_rows, s_rows, r_rows, x_rows):
    complex_rows(r_rows, g_rows, s_rows, None)
    complex_rows(x_rows, r_rows, g_rows, g_rows)
    complex_rows(s_rows, r_rows, x_rows, g_rows)


def scatter_kernel(
    green, phonon_in, lags_in, grad_in, neighbor_in, kept,
    held, phonon, lags, grad, neighbor,
    swap_out, swap_in, late_out, late_in, stage, got, result, back,
    whi, wlo, khi, klo, factors, fhi, flo, partial, summed, early, g_rows, s_rows, r_rows, x_rows,
    send_sems, recv_sems, stage_sem, load_sem, small_sem, keep_sem,
):
    z, y, x, core = coordinates()
    position = (z, y, x)
    parities = (x % 2, 1 - x % 2)
    sibling = {"mom": 1 - core}
    column, plane = neighbours(z, y, x)
    barrier = pltpu.get_barrier_semaphore()
    for device in [sibling] + plane + column:
        signal(barrier, device)
    loads = load_columns(green, held, load_sem)
    smalls = [
        pltpu.make_async_copy(source, target, small_sem.at[i])
        for i, (source, target) in enumerate(
            [(phonon_in, phonon), (lags_in, lags), (grad_in, grad), (neighbor_in, neighbor)]
        )
    ]
    for small in smalls:
        small.start()

    def channel(i):
        return send_sems.at[i], recv_sems.at[i]

    def swap_of(half, source, target, i):
        return pltpu.make_async_remote_copy(
            src_ref=source.at[half],
            dst_ref=target.at[half],
            send_sem=send_sems.at[i + half],
            recv_sem=recv_sems.at[i + half],
            device_id=sibling,
            device_id_type=MESH,
        )

    for load in loads:
        load.wait()
    for half, s in enumerate(parities):
        for zh in range(2):
            for t in range(4):
                swap_out[half, zh * 4 + t] = held[atom_rows(t, s, zh, 1 - core), :]
    pl.semaphore_wait(barrier, 23)

    swaps = [swap_of(half, swap_out, swap_in, 0) for half in range(2)]
    for swap in swaps:
        swap.start()
    for device in column:
        signal(stage_sem, device)
    for t in range(4):
        stage[pl.ds(core * 4 + t, PAIRS, stride=8), :] = held[
            pl.ds(t * 256 + core, PAIRS, stride=2), :
        ]
    pl.semaphore_wait(stage_sem, 7)
    for half, s in enumerate(parities):
        swaps[half].wait()
        for zh in range(2):
            for t in range(4):
                stage[energy_rows(s, zh, 1 - core, t), :] = swap_in[half, zh * 4 + t]
        exchange_start(position, half, stage, got, *channel(2 + half))

    for small in smalls:
        small.wait()
    build_weights(core, phonon, lags, whi, wlo)
    build_kron(core, neighbor, grad, khi, klo, factors)

    def keep(i, source):
        copy = pltpu.make_async_copy(source, kept.at[i], keep_sem.at[i])
        copy.start()
        return copy

    pick_half(held, r_rows, parities[1])
    turn(r_rows, x_rows)
    keeps = [keep(0, x_rows)]
    pick_half(held, s_rows, parities[0])
    turn(s_rows, g_rows)

    exchange_descriptor(0, stage, got, *channel(2), sibling).wait()
    sandwich_half(parities[0], got, khi, klo, fhi, flo)
    for out in range(2):
        rows = slice(out * 128, out * 128 + 128)
        partial[rows, :] = mix_half(rows, parities[0], whi, wlo, fhi, flo)
    exchange_descriptor(1, stage, got, *channel(3), sibling).wait()
    sandwich_half(parities[1], got, khi, klo, fhi, flo)
    for half, s in enumerate(parities):
        rows = pl.ds(pl.multiple_of(s * 128, 128), 128)
        total = partial[rows, :] + mix_half(rows, parities[1], whi, wlo, fhi, flo)
        for k in range(2):
            for zh in range(2):
                first = k * 64 + zh * 32
                for t in range(4):
                    result[energy_rows(s, zh, k, t), :] = total[
                        first : first + 32, t * 128 : t * 128 + 128
                    ]
        exchange_start(position, half, result, back, *channel(4 + half))

    keeps[0].wait()
    for half, s in enumerate(parities):
        exchange_descriptor(half, result, back, *channel(4 + half), sibling).wait()
        for zh in range(2):
            for t in range(4):
                late_out[half, zh * 4 + t] = back[energy_rows(s, zh, 1 - core, t), :]
        swap_back = swap_of(half, late_out, late_in, 6)
        swap_back.start()
        for zh in range(2):
            for t in range(4):
                summed[half, block_rows(t, zh, core), :] = back[energy_rows(s, zh, core, t), :]
        swap_back.wait()
        for zh in range(2):
            for t in range(4):
                summed[half, block_rows(t, zh, 1 - core), :] = late_in[half, zh * 4 + t]
        keeps.append(keep(1 + half, summed.at[half]))
        if half == 0:
            turn(summed.at[0], s_rows)
            dyson_rows(g_rows, s_rows, r_rows, x_rows)
            turn(s_rows, early)
            keeps.append(keep(3, early))
    for copy in keeps[1:]:
        copy.wait()


def scatter(green, phonon, lags, grad, neighbor):
    column = pltpu.VMEM((1024, 128), F32)
    half = pltpu.VMEM((512, 128), F32)
    swapped = pltpu.VMEM((2, 8, 32, 128), F32)
    return pl.pallas_call(
        scatter_kernel,
        out_shape=jax.ShapeDtypeStruct((4, 512, 128), F32),
        in_specs=[pl.BlockSpec(memory_space=pltpu.HBM)] * 5,
        out_specs=pl.BlockSpec(memory_space=pltpu.HBM),
        scratch_shapes=[
            column,
            pltpu.VMEM((2, 256), F32),
            pltpu.VMEM((1, 32), jnp.int32),
            pltpu.VMEM((64, 256), F32),
            pltpu.SMEM((2, 4), jnp.int32),
            swapped,
            swapped,
            swapped,
            swapped,
            column,
            column,
            column,
            column,
            pltpu.VMEM((2, 256, 512), BF16),
            pltpu.VMEM((2, 256, 512), BF16),
            pltpu.VMEM((1024, 256), BF16),
            pltpu.VMEM((1024, 256), BF16),
            pltpu.VMEM((64, 256), F32),
            pltpu.VMEM((512, 512), BF16),
            pltpu.VMEM((512, 512), BF16),
            pltpu.VMEM((256, 512), F32),
            pltpu.VMEM((2, 512, 128), F32),
            half,
            half,
            half,
            half,
            half,
            pltpu.SemaphoreType.DMA((8,)),
            pltpu.SemaphoreType.DMA((8,)),
            pltpu.SemaphoreType.REGULAR,
            pltpu.SemaphoreType.DMA((4,)),
            pltpu.SemaphoreType.DMA((4,)),
            pltpu.SemaphoreType.DMA((4,)),
        ],
        compiler_params=pltpu.CompilerParams(
            collective_id=0, has_side_effects=True, vmem_limit_bytes=56 * 1024 * 1024
        ),
        cost_estimate=pl.CostEstimate(
            flops=2 * 10**9, bytes_accessed=4 * 10**6, transcendentals=0
        ),
    )(green, phonon, lags, grad, neighbor)


def complex_rows(target, left, right, base):
    @pl.loop(0, 4)
    def _(block):
        first = pl.multiple_of(block * 64, 64)
        real = [None] * 4
        imag = [None] * 4
        for j in range(16):
            b_real = right[j * 16 : j * 16 + 16, :]
            b_imag = right[256 + j * 16 : 256 + j * 16 + 16, :]
            for i in range(4):
                a_real = left[pl.ds(first + i * 16 + j, 1), :]
                a_imag = left[pl.ds(256 + first + i * 16 + j, 1), :]
                add_real = a_real * b_real - a_imag * b_imag
                add_imag = a_real * b_imag + a_imag * b_real
                real[i] = add_real if j == 0 else real[i] + add_real
                imag[i] = add_imag if j == 0 else imag[i] + add_imag
        for i in range(4):
            rows = pl.ds(first + i * 16, 16)
            late = pl.ds(256 + first + i * 16, 16)
            if base is None:
                target[rows, :] = real[i]
                target[late, :] = imag[i]
            else:
                target[rows, :] = base[rows, :] + real[i]
                target[late, :] = base[late, :] + imag[i]


def store_columns(source, target, sems):
    stores = [
        pltpu.make_async_copy(
            source.at[pl.ds(t * 256, 256)], target.at[:, pl.ds(t * 128, 128)], sems.at[t]
        )
        for t in range(4)
    ]
    for store in stores:
        store.start()
    return stores


def dyson_kernel(
    kept, sigma, after, held, turned, summed, final, s_rows, r_rows, x_rows,
    load_sem, sigma_sem, after_sem,
):
    soon = lax.axis_index("energy") % 2
    loads = [
        pltpu.make_async_copy(kept.at[i], held.at[i], load_sem.at[i]) for i in (2, 0, 1, 3)
    ]
    for load in loads:
        load.start()
    loads[0].wait()
    turn(held.at[2], s_rows)
    place_half(held.at[2], summed, 1 - soon)
    loads[2].wait()
    place_half(held.at[1], summed, soon)
    stores = store_columns(summed, sigma, sigma_sem)
    loads[1].wait()
    dyson_rows(held.at[0], s_rows, r_rows, x_rows)
    loads[3].wait()
    place_half(held.at[3], final, soon)
    turn(s_rows, turned)
    place_half(turned, final, 1 - soon)
    stores += store_columns(final, after, after_sem)
    for store in stores:
        store.wait()


def dyson(kept):
    whole = pl.BlockSpec(memory_space=pltpu.HBM)
    half = pltpu.VMEM((512, 128), F32)
    return pl.pallas_call(
        dyson_kernel,
        out_shape=[jax.ShapeDtypeStruct((256, 512), F32)] * 2,
        in_specs=[whole],
        out_specs=[whole] * 2,
        scratch_shapes=[pltpu.VMEM((4, 512, 128), F32), half]
        + [pltpu.VMEM((1024, 128), F32)] * 2
        + [half] * 3
        + [pltpu.SemaphoreType.DMA((4,))] * 3,
        compiler_params=pltpu.CompilerParams(vmem_limit_bytes=56 * 1024 * 1024),
        cost_estimate=pl.CostEstimate(
            flops=3 * 10**7, bytes_accessed=2 * 10**6, transcendentals=0
        ),
    )(kept)


def body(green, phonon, lag_offsets, grad_table, neighbor_grad):
    own = green.reshape(256, 512)
    kept = scatter(own, phonon, lag_offsets.reshape(1, 32), grad_table, neighbor_grad)
    sigma, after = dyson(kept)
    return sigma.reshape(green.shape), after.reshape(green.shape)


def solution(mesh):
    whole = P("mom", ("energy", "tile"), None, None)
    rows = P(("energy", "tile"), None)
    return jax.shard_map(
        body,
        mesh=mesh,
        in_specs=(whole, rows, P(), P(), rows),
        out_specs=(whole, whole),
        check_vma=False,
    )
```

time: 56.1 us -> 51.5 us (0.918)
  local copies, waits for them, and re-layouts: 2.55 us -> 0 us
  Pallas kernels: 52.6 us -> 50.8 us
    unnamed x10 -> x0, local copies, waits for them, and re-layouts: 2.55 us -> none
    pallas_call x1, Pallas kernels: 5.29 us -> 3.97 us  [dyson(): pl.pallas_call(dyson_kernel, out_shape=[jax.ShapeDtypeStruct((256, 512),...]
where the time goes in v1:
time: 51.5 us; the launch traced here: 51.4 us
  Pallas kernels  50.8 us (99%)
  between operations  0.64 us (1%)
    pallas_call x1, Pallas kernels, scatter(): pl.pallas_call(scatter_kernel, out_shape=jax.ShapeDtypeStruct((4, 512, 12...  46.8 us
    pallas_call x1, Pallas kernels, dyson(): pl.pallas_call(dyson_kernel, out_shape=[jax.ShapeDtypeStruct((256, 512),...  3.97 us

profile of v1, /device:TPU:1, one launch (start us, length us, event | category | flops | bytes accessed | tf_op | source)
XLA Modules:
  0.0 51.4 jit_solution(14318367048395798745)
XLA Ops:
  0.6 46.8 %shard_map.68.kept = f32[4,512,128]{2,1,0:T(8,128)} custom-call(f32[256,512]{1,0:T(8,128)} %bitcast.4, f32[2,256]{1,0:T(2,128)} %phonon_in.1, s32[1,32]{1,0:T(1,128)} %bitcast.7, f32[64,256]{1,0:T(8,128)} %grad_in.1, s32[2,4]{1,0:T(2,128)} %neighbor_in.1), custom_call_target="tpu_custom_call" | custom-call | flops 2000000000 | bytes 4000000 | tf_op jit(solution)/shard_map/pallas_call | solution.py:385
  47.4 4.0 %shard_map.69 = (f32[256,512]{1,0:T(8,128)}, f32[256,512]{1,0:T(8,128)}) custom-call(f32[4,512,128]{2,1,0:T(8,128)} %shard_map.68.kept), custom_call_target="tpu_custom_call" | custom-call | flops 30000000 | bytes 2000000 | tf_op jit(solution)/shard_map/pallas_call | solution.py:503

commit v2 on v1

--- a/solution.py
+++ b/solution.py
@@ -71,16 +71,19 @@
             device_id_type=MESH,
         ).start()
 
+    def plane(k):
+        yy = (y + 2 + k // 2) % 4
+        xx = (x + half + 2 * ((k + 1) % 2)) % 4
+        for zz in depth:
+            send(zz, yy, xx)
+
     if half == 0:
+        pl.loop(0, 5)(plane)
+        pl.loop(6, 8)(plane)
         for zz in depth[1:]:
             send(zz, y, x)
-
-    @pl.loop(1 - half, 8)
-    def _(k):
-        yy = (y + k // 2) % 4
-        xx = (x + half + 2 * (k % 2)) % 4
-        for zz in depth:
-            send(zz, yy, xx)
+    else:
+        pl.loop(0, 8)(plane)
 
     if half == 0:
         landing[here, :] = source[here, :]

time: 51.5 us -> 51.1 us (level)
  no operation moved by 1% of the time
where the time goes in v2:
time: 51.1 us; the launch traced here: 50.9 us
  Pallas kernels  50.3 us (98%)
  between operations  0.64 us (1%)
    pallas_call x1, Pallas kernels, scatter(): pl.pallas_call(scatter_kernel, out_shape=jax.ShapeDtypeStruct((4, 512, 12...  46.3 us
    pallas_call x1, Pallas kernels, dyson(): pl.pallas_call(dyson_kernel, out_shape=[jax.ShapeDtypeStruct((256, 512),...  3.97 us

profile of v2, /device:TPU:1, one launch (start us, length us, event | category | flops | bytes accessed | tf_op | source)
XLA Modules:
  0.0 50.9 jit_solution(6844068541444698023)
XLA Ops:
  0.6 46.3 %shard_map.68.kept = f32[4,512,128]{2,1,0:T(8,128)} custom-call(f32[256,512]{1,0:T(8,128)} %bitcast.4, f32[2,256]{1,0:T(2,128)} %phonon_in.1, s32[1,32]{1,0:T(1,128)} %bitcast.7, f32[64,256]{1,0:T(8,128)} %grad_in.1, s32[2,4]{1,0:T(2,128)} %neighbor_in.1), custom_call_target="tpu_custom_call" | custom-call | flops 2000000000 | bytes 4000000 | tf_op jit(solution)/shard_map/pallas_call | solution.py:388
  47.0 4.0 %shard_map.69 = (f32[256,512]{1,0:T(8,128)}, f32[256,512]{1,0:T(8,128)}) custom-call(f32[4,512,128]{2,1,0:T(8,128)} %shard_map.68.kept), custom_call_target="tpu_custom_call" | custom-call | flops 30000000 | bytes 2000000 | tf_op jit(solution)/shard_map/pallas_call | solution.py:506

commit v3 on v2

--- a/solution.py
+++ b/solution.py
@@ -259,7 +259,7 @@
 
 
 def scatter_kernel(
-    green, phonon_in, lags_in, grad_in, neighbor_in, kept,
+    green, phonon_in, lags_in, grad_in, neighbor_in, kept, late,
     held, phonon, lags, grad, neighbor,
     swap_out, swap_in, late_out, late_in, stage, got, result, back,
     whi, wlo, khi, klo, factors, fhi, flo, partial, summed, early, g_rows, s_rows, r_rows, x_rows,
@@ -362,21 +362,39 @@
         for zh in range(2):
             for t in range(4):
                 late_out[half, zh * 4 + t] = back[energy_rows(s, zh, 1 - core, t), :]
+        if half == 1:
+            break
         swap_back = swap_of(half, late_out, late_in, 6)
         swap_back.start()
         for zh in range(2):
             for t in range(4):
-                summed[half, block_rows(t, zh, core), :] = back[energy_rows(s, zh, core, t), :]
+                summed[block_rows(t, zh, core), :] = back[energy_rows(s, zh, core, t), :]
         swap_back.wait()
         for zh in range(2):
             for t in range(4):
-                summed[half, block_rows(t, zh, 1 - core), :] = late_in[half, zh * 4 + t]
-        keeps.append(keep(1 + half, summed.at[half]))
-        if half == 0:
-            turn(summed.at[0], s_rows)
-            dyson_rows(g_rows, s_rows, r_rows, x_rows)
-            turn(s_rows, early)
-            keeps.append(keep(3, early))
+                summed[block_rows(t, zh, 1 - core), :] = late_in[half, zh * 4 + t]
+        keeps.append(keep(1, summed))
+        turn(summed, s_rows)
+        dyson_rows(g_rows, s_rows, r_rows, x_rows)
+        turn(s_rows, early)
+        keeps.append(keep(2, early))
+
+    swap_late = pltpu.make_async_remote_copy(
+        src_ref=late_out.at[1],
+        dst_ref=late.at[core],
+        send_sem=send_sems.at[7],
+        recv_sem=recv_sems.at[7],
+        device_id=sibling,
+        device_id_type=MESH,
+    )
+    swap_late.start()
+    for zh in range(2):
+        for t in range(4):
+            late_in[1, zh * 4 + t] = back[energy_rows(parities[1], zh, core, t), :]
+    own_late = pltpu.make_async_copy(late_in.at[1], late.at[core], keep_sem.at[3])
+    own_late.start()
+    own_late.wait()
+    swap_late.wait()
     for copy in keeps[1:]:
         copy.wait()
 
@@ -387,9 +405,12 @@
     swapped = pltpu.VMEM((2, 8, 32, 128), F32)
     return pl.pallas_call(
         scatter_kernel,
-        out_shape=jax.ShapeDtypeStruct((4, 512, 128), F32),
+        out_shape=[
+            jax.ShapeDtypeStruct((3, 512, 128), F32),
+            jax.ShapeDtypeStruct((2, 8, 32, 128), F32),
+        ],
         in_specs=[pl.BlockSpec(memory_space=pltpu.HBM)] * 5,
-        out_specs=pl.BlockSpec(memory_space=pltpu.HBM),
+        out_specs=[pl.BlockSpec(memory_space=pltpu.HBM)] * 2,
         scratch_shapes=[
             column,
             pltpu.VMEM((2, 256), F32),
@@ -412,7 +433,7 @@
             pltpu.VMEM((512, 512), BF16),
             pltpu.VMEM((512, 512), BF16),
             pltpu.VMEM((256, 512), F32),
-            pltpu.VMEM((2, 512, 128), F32),
+            half,
             half,
             half,
             half,
@@ -474,25 +495,30 @@
 
 
 def dyson_kernel(
-    kept, sigma, after, held, turned, summed, final, s_rows, r_rows, x_rows,
+    kept, late, sigma, after, held, ended, turned, summed, final, s_rows, r_rows, x_rows,
     load_sem, sigma_sem, after_sem,
 ):
     soon = lax.axis_index("energy") % 2
-    loads = [
-        pltpu.make_async_copy(kept.at[i], held.at[i], load_sem.at[i]) for i in (2, 0, 1, 3)
-    ]
+    first = pltpu.make_async_copy(late, ended, load_sem.at[3])
+    first.start()
+    loads = [pltpu.make_async_copy(kept.at[i], held.at[i], load_sem.at[i]) for i in range(3)]
     for load in loads:
         load.start()
-    loads[0].wait()
-    turn(held.at[2], s_rows)
-    place_half(held.at[2], summed, 1 - soon)
-    loads[2].wait()
+    first.wait()
+    for t in range(4):
+        block = jnp.concatenate(
+            [ended[parity, zh * 4 + t] for zh in range(2) for parity in range(2)], axis=0
+        )
+        s_rows[t * 128 : t * 128 + 128, :] = block.T
+    for t, zh, parity in QUARTERS:
+        summed[atom_rows(t, 1 - soon, zh, parity), :] = ended[parity, zh * 4 + t]
+    loads[1].wait()
     place_half(held.at[1], summed, soon)
     stores = store_columns(summed, sigma, sigma_sem)
-    loads[1].wait()
+    loads[0].wait()
     dyson_rows(held.at[0], s_rows, r_rows, x_rows)
-    loads[3].wait()
-    place_half(held.at[3], final, soon)
+    loads[2].wait()
+    place_half(held.at[2], final, soon)
     turn(s_rows, turned)
     place_half(turned, final, 1 - soon)
     stores += store_columns(final, after, after_sem)
@@ -500,15 +526,19 @@
         store.wait()
 
 
-def dyson(kept):
+def dyson(kept, late):
     whole = pl.BlockSpec(memory_space=pltpu.HBM)
     half = pltpu.VMEM((512, 128), F32)
     return pl.pallas_call(
         dyson_kernel,
         out_shape=[jax.ShapeDtypeStruct((256, 512), F32)] * 2,
-        in_specs=[whole],
+        in_specs=[whole] * 2,
         out_specs=[whole] * 2,
-        scratch_shapes=[pltpu.VMEM((4, 512, 128), F32), half]
+        scratch_shapes=[
+            pltpu.VMEM((3, 512, 128), F32),
+            pltpu.VMEM((2, 8, 32, 128), F32),
+            half,
+        ]
         + [pltpu.VMEM((1024, 128), F32)] * 2
         + [half] * 3
         + [pltpu.SemaphoreType.DMA((4,))] * 3,
@@ -516,13 +546,13 @@
         cost_estimate=pl.CostEstimate(
             flops=3 * 10**7, bytes_accessed=2 * 10**6, transcendentals=0
         ),
-    )(kept)
+    )(kept, late)
 
 
 def body(green, phonon, lag_offsets, grad_table, neighbor_grad):
     own = green.reshape(256, 512)
-    kept = scatter(own, phonon, lag_offsets.reshape(1, 32), grad_table, neighbor_grad)
-    sigma, after = dyson(kept)
+    held = scatter(own, phonon, lag_offsets.reshape(1, 32), grad_table, neighbor_grad)
+    sigma, after = dyson(*held)
     return sigma.reshape(green.shape), after.reshape(green.shape)
 
 

time: 51.1 us -> 50.5 us (0.988)
  Pallas kernels: 50.3 us -> 49.7 us
    pallas_call x1, Pallas kernels: 46.3 us -> 45.8 us  [scatter(): pl.pallas_call(scatter_kernel, out_shape=[jax.ShapeDtypeStruct((3, 512, 1...]
where the time goes in v3:
time: 50.5 us; the launch traced here: 50.4 us
  Pallas kernels  49.7 us (98%)
  between operations  0.64 us (1%)
    pallas_call x1, Pallas kernels, scatter(): pl.pallas_call(scatter_kernel, out_shape=[jax.ShapeDtypeStruct((3, 512, 1...  45.8 us
    pallas_call x1, Pallas kernels, dyson(): pl.pallas_call(dyson_kernel, out_shape=[jax.ShapeDtypeStruct((256, 512),...  3.97 us

profile of v3, /device:TPU:1, one launch (start us, length us, event | category | flops | bytes accessed | tf_op | source)
XLA Modules:
  0.0 50.4 jit_solution(9781390548965948660)
XLA Ops:
  0.6 45.8 %shard_map.68 = (f32[3,512,128]{2,1,0:T(8,128)}, f32[2,8,32,128]{3,2,1,0:T(8,128)}) custom-call(f32[256,512]{1,0:T(8,128)} %bitcast.4, f32[2,256]{1,0:T(2,128)} %phonon_in.1, s32[1,32]{1,0:T(1,128)} %bitcast.7, f32[64,256]{1,0:T(8,128)} %grad_in.1, s32[2,4]{1,0:T(2,128)} %neighbor_in.1), custom_call_target="tpu_custom_call" | custom-call | flops 2000000000 | bytes 4000000 | tf_op jit(solution)/shard_map/pallas_call | solution.py:406
  46.4 4.0 %shard_map.69 = (f32[256,512]{1,0:T(8,128)}, f32[256,512]{1,0:T(8,128)}) custom-call(f32[3,512,128]{2,1,0:T(8,128)} %get-tuple-element.6.kept, f32[2,8,32,128]{3,2,1,0:T(8,128)} %get-tuple-element.7.late), custom_call_target="tpu_custom_call" | custom-call | flops 30000000 | bytes 2000000 | tf_op jit(solution)/shard_map/pallas_call | solution.py:532

commit v4 on v3

--- a/solution.py
+++ b/solution.py
@@ -241,13 +241,14 @@
         target[block_rows(t, zh, parity), :] = source[atom_rows(t, s, zh, parity), :]
 
 
-def place_half(source, target, s):
+def place_half(source, target, s, tiles=range(4)):
     for t, zh, parity in QUARTERS:
-        target[atom_rows(t, s, zh, parity), :] = source[block_rows(t, zh, parity), :]
-
-
-def turn(source, target):
-    for t in range(4):
+        if t in tiles:
+            target[atom_rows(t, s, zh, parity), :] = source[block_rows(t, zh, parity), :]
+
+
+def turn(source, target, tiles=range(4)):
+    for t in tiles:
         rows = slice(t * 128, t * 128 + 128)
         target[rows, :] = source[rows, :].T
 
@@ -455,8 +456,8 @@
     )(green, phonon, lags, grad, neighbor)
 
 
-def complex_rows(target, left, right, base):
-    @pl.loop(0, 4)
+def complex_rows(target, left, right, base, blocks=(0, 4)):
+    @pl.loop(*blocks)
     def _(block):
         first = pl.multiple_of(block * 64, 64)
         real = [None] * 4
@@ -482,12 +483,12 @@
                 target[late, :] = base[late, :] + imag[i]
 
 
-def store_columns(source, target, sems):
+def store_columns(source, target, sems, tiles=range(4)):
     stores = [
         pltpu.make_async_copy(
             source.at[pl.ds(t * 256, 256)], target.at[:, pl.ds(t * 128, 128)], sems.at[t]
         )
-        for t in range(4)
+        for t in tiles
     ]
     for store in stores:
         store.start()
@@ -516,12 +517,16 @@
     place_half(held.at[1], summed, soon)
     stores = store_columns(summed, sigma, sigma_sem)
     loads[0].wait()
-    dyson_rows(held.at[0], s_rows, r_rows, x_rows)
+    g_rows = held.at[0]
+    complex_rows(r_rows, g_rows, s_rows, None)
+    complex_rows(x_rows, r_rows, g_rows, g_rows)
     loads[2].wait()
     place_half(held.at[2], final, soon)
-    turn(s_rows, turned)
-    place_half(turned, final, 1 - soon)
-    stores += store_columns(final, after, after_sem)
+    for i in range(2):
+        complex_rows(s_rows, r_rows, x_rows, g_rows, (2 * i, 2 * i + 2))
+        turn(s_rows, turned, (i, i + 2))
+        place_half(turned, final, 1 - soon, (i, i + 2))
+        stores += store_columns(final, after, after_sem, (i, i + 2))
     for store in stores:
         store.wait()
 

time: 50.5 us -> 50.5 us (level)
  no operation moved by 1% of the time
where the time goes in v4:
time: 50.5 us; the launch traced here: 50.4 us
  Pallas kernels  49.8 us (99%)
  between operations  0.64 us (1%)
    pallas_call x1, Pallas kernels, scatter(): pl.pallas_call(scatter_kernel, out_shape=[jax.ShapeDtypeStruct((3, 512, 1...  45.8 us
    pallas_call x1, Pallas kernels, dyson(): pl.pallas_call(dyson_kernel, out_shape=[jax.ShapeDtypeStruct((256, 512),...  3.98 us

profile of v4, /device:TPU:1, one launch (start us, length us, event | category | flops | bytes accessed | tf_op | source)
XLA Modules:
  0.0 50.4 jit_solution(15297488172588198850)
XLA Ops:
  0.6 45.8 %shard_map.68 = (f32[3,512,128]{2,1,0:T(8,128)}, f32[2,8,32,128]{3,2,1,0:T(8,128)}) custom-call(f32[256,512]{1,0:T(8,128)} %bitcast.4, f32[2,256]{1,0:T(2,128)} %phonon_in.1, s32[1,32]{1,0:T(1,128)} %bitcast.7, f32[64,256]{1,0:T(8,128)} %grad_in.1, s32[2,4]{1,0:T(2,128)} %neighbor_in.1), custom_call_target="tpu_custom_call" | custom-call | flops 2000000000 | bytes 4000000 | tf_op jit(solution)/shard_map/pallas_call | solution.py:407
  46.4 4.0 %shard_map.69 = (f32[256,512]{1,0:T(8,128)}, f32[256,512]{1,0:T(8,128)}) custom-call(f32[3,512,128]{2,1,0:T(8,128)} %get-tuple-element.6.kept, f32[2,8,32,128]{3,2,1,0:T(8,128)} %get-tuple-element.7.late), custom_call_target="tpu_custom_call" | custom-call | flops 30000000 | bytes 2000000 | tf_op jit(solution)/shard_map/pallas_call | solution.py:537
